TPU v7x, 256 devices: a whole 4x4x8 slice. The times are simulated.
256 devices in a mesh: seq: 64 (over x, z, core), tp: 4 (over y).
Axes of the slice: x: 4, y: 4, z: 8, core: 2. Of those that a mesh axis runs over, the one named last changes fastest.
Arguments:
- hidden_in: bfloat16 [256, 2048], P('seq'), may hold values from -6 to 6
- query_weight: bfloat16 [2048, 2048], P(None, 'tp'), may hold values from -0.125 to 0.125
- key_weight: bfloat16 [2048, 2048], P(None, 'tp'), may hold values from -0.125 to 0.125
- value_weight: bfloat16 [2048, 2048], P(None, 'tp'), may hold values from -0.125 to 0.125
- out_weight: bfloat16 [2048, 2048], P('tp'), may hold values from -0.125 to 0.125
- query_gain: float32 [2048], P('tp'), may hold values from 0.5 to 1.5
- key_gain: float32 [2048], P('tp'), may hold values from 0.5 to 1.5
- post_gain: float32 [2048], P('tp'), may hold values from 0.5 to 1.5
- key_cache: bfloat16 [4, 8192, 2048], P(None, 'seq', 'tp'), may hold values from -110 to 110
- value_cache: bfloat16 [4, 8192, 2048], P(None, 'seq', 'tp'), may hold values from -6 to 6
- cache_lengths: int32 [4], replicated, may hold values from 1024 to 8128
- parents: int32 [4, 64], replicated, may hold values from -1 to 62, as said below
- accepted_leaf: int32 [4], replicated, may hold values from 0 to 63
Outputs:
- hidden_out: bfloat16 [256, 2048], P('seq', 'tp')
- new_key_cache: bfloat16 [4, 8192, 2048], P(None, 'seq', 'tp')
- new_value_cache: bfloat16 [4, 8192, 2048], P(None, 'seq', 'tp')
Inputs may be any that keep to these rules, and one draw needn't show every extreme that they name: parents[r, 0] = -1; for i >= 1, parents[r, i] lies in max(0, i - 3) to i - 1; parents[r, 63] = 62.
All inputs are finite; a program needn't handle non-finite values.
Results may differ from a plain program's by a relative error of at most 0.019.
Values may be sent and summed in bfloat16 or wider, within the bound.
A program may use at most 128 MiB of HBM per device.

v0:
```python
import math
import jax
import jax.numpy as jnp
from jax import lax
from jax.sharding import PartitionSpec as P

HEAD_DIM = 128
EPS = 1e-06
THETA = 500000.0
NEG = -1e30


def joined_2(x, axis, combine):
    everything = jax.tree.map(lambda part: lax.all_gather(part, axis), x)
    initial = jax.tree.map(lambda part: part[0], everything)

    def step(k, so_far):
        return combine(so_far, jax.tree.map(lambda part: part[k], everything))

    return lax.fori_loop(1, lax.axis_size(axis), step, initial)


def ancestry(parents):
    number = parents.shape[-1]
    columns = jnp.arange(number, dtype=jnp.int32)
    single = (parents[:, :, None] == columns[None, None, :]).astype(jnp.float32)
    ancestors = jnp.eye(number, dtype=jnp.float32)[None] + single
    for repeat in range(max(1, (number - 1).bit_length())):
        ancestors = jnp.minimum(
            jnp.einsum("rij,rjk->rik", ancestors, ancestors, precision=lax.Precision.HIGHEST), 1.0
        )
    tree_depth = jnp.sum(ancestors, axis=-1) - 1.0
    return (ancestors, tree_depth)


def rotary(values, positions):
    half_dim = values.shape[-1] // 2
    freqs = THETA ** (-2.0 * jnp.arange(half_dim, dtype=jnp.float32) / values.shape[-1])
    angles = positions[:, None, None] * freqs[None, None, :]
    cosine = jnp.cos(angles)
    sine = jnp.sin(angles)
    first = values[..., :half_dim]
    second = values[..., half_dim:]
    return jnp.concatenate(
        [first * cosine - second * sine, second * cosine + first * sine], axis=-1
    )


def prepare(raw, square_sum, gain, positions, width_all):
    scaled = raw * lax.rsqrt(square_sum / width_all + EPS)[:, None] * gain[None, :]
    rows_here = raw.shape[0]
    heads_here = raw.shape[1] // HEAD_DIM
    turned = rotary(scaled.reshape(rows_here, heads_here, HEAD_DIM), positions)
    return turned.reshape(rows_here, heads_here * HEAD_DIM).astype(jnp.bfloat16)


def join_partials(first, second):
    peak_first, total_first, out_first = first
    peak_second, total_second, out_second = second
    highest = jnp.maximum(peak_first, peak_second)
    scale_first = jnp.exp(peak_first - highest)
    scale_second = jnp.exp(peak_second - highest)
    rows_here, heads_here = highest.shape
    joined = (
        out_first.reshape(rows_here, heads_here, -1) * scale_first[..., None]
        + out_second.reshape(rows_here, heads_here, -1) * scale_second[..., None]
    )
    return (
        highest,
        total_first * scale_first + total_second * scale_second,
        joined.reshape(out_first.shape),
    )


def body(
    hidden_in,
    query_weight,
    key_weight,
    value_weight,
    out_weight,
    query_gain,
    key_gain,
    post_gain,
    key_cache,
    value_cache,
    cache_lengths,
    parents,
    accepted_leaf,
):
    requests, block, local_width = key_cache.shape
    draft = parents.shape[1]
    tokens = requests * draft
    own_rows = hidden_in.shape[0]
    model_width = hidden_in.shape[1]
    heads_here = local_width // HEAD_DIM
    full_width = local_width * lax.axis_size("tp")
    seq_index = lax.axis_index("seq")
    tp_index = lax.axis_index("tp")
    row_start = seq_index * own_rows
    ancestors, tree_depth = ancestry(parents)
    positions = (cache_lengths[:, None].astype(jnp.float32) + tree_depth).reshape(tokens)
    piece = lax.all_gather(hidden_in, "seq", axis=0, tiled=True)
    raw = jnp.concatenate(
        [
            jnp.dot(piece, query_weight, preferred_element_type=jnp.float32),
            jnp.dot(piece, key_weight, preferred_element_type=jnp.float32),
            jnp.dot(piece, value_weight, preferred_element_type=jnp.float32),
        ],
        axis=1,
    )
    query_raw = raw[:, :local_width]
    key_raw = raw[:, local_width : 2 * local_width]
    value_raw = raw[:, 2 * local_width :]
    query_square, key_square = lax.psum(
        (jnp.sum(query_raw * query_raw, axis=1), jnp.sum(key_raw * key_raw, axis=1)), "tp"
    )
    queries = prepare(query_raw, query_square, query_gain, positions, full_width)
    keys = prepare(key_raw, key_square, key_gain, positions, full_width)
    values = value_raw.astype(jnp.bfloat16)
    factor = 1.0 / math.sqrt(HEAD_DIM)
    query_blocks = queries.reshape(requests, draft, heads_here, HEAD_DIM)
    cache_keys = key_cache.reshape(requests, block, heads_here, HEAD_DIM)
    cache_values = value_cache.reshape(requests, block, heads_here, HEAD_DIM)
    places = seq_index * block + jnp.arange(block, dtype=jnp.int32)
    cache_scores = (
        jnp.einsum("rihd,rlhd->rihl", query_blocks, cache_keys, preferred_element_type=jnp.float32)
        * factor
    )
    visible = (places[None, :] < cache_lengths[:, None])[:, None, None, :]
    cache_scores = jnp.where(visible, cache_scores, NEG)
    cache_peak = jnp.max(cache_scores, axis=-1)
    cache_weights = jnp.where(visible, jnp.exp(cache_scores - cache_peak[..., None]), 0.0)
    cache_total = jnp.sum(cache_weights, axis=-1).reshape(tokens, heads_here)
    cache_out = jnp.einsum(
        "rihl,rlhd->rihd",
        cache_weights,
        cache_values.astype(jnp.float32),
        precision=lax.Precision.HIGHEST,
    ).reshape(tokens, local_width)
    cache_peak = cache_peak.reshape(tokens, heads_here)
    request_now = row_start // draft
    own_queries_all = lax.dynamic_slice_in_dim(queries, row_start, own_rows).reshape(
        own_rows, heads_here, HEAD_DIM
    )
    request_keys = lax.dynamic_index_in_dim(
        keys.reshape(requests, draft, local_width), request_now, 0, keepdims=False
    ).reshape(draft, heads_here, HEAD_DIM)
    request_values = lax.dynamic_index_in_dim(
        values.reshape(requests, draft, local_width), request_now, 0, keepdims=False
    ).reshape(draft, heads_here, HEAD_DIM)
    tree_rows = lax.dynamic_slice_in_dim(ancestors.reshape(tokens, draft), row_start, own_rows)
    draft_scores = (
        jnp.einsum(
            "ihd,jhd->ihj", own_queries_all, request_keys, preferred_element_type=jnp.float32
        )
        * factor
    )
    tree_mask = (tree_rows > 0.5)[:, None, :]
    draft_scores = jnp.where(tree_mask, draft_scores, NEG)
    draft_peak = jnp.max(draft_scores, axis=-1)
    draft_weights = jnp.where(tree_mask, jnp.exp(draft_scores - draft_peak[..., None]), 0.0)
    draft_total = jnp.sum(draft_weights, axis=-1)
    draft_out = jnp.einsum(
        "ihj,jhd->ihd",
        draft_weights,
        request_values.astype(jnp.float32),
        precision=lax.Precision.HIGHEST,
    ).reshape(own_rows, local_width)
    merged = joined_2((cache_peak, cache_total, cache_out), "seq", join_partials)
    mine = tuple((lax.dynamic_slice_in_dim(member, row_start, own_rows) for member in merged))
    highest, denominator, summed = join_partials(mine, (draft_peak, draft_total, draft_out))
    attention = (
        (summed.reshape(own_rows, heads_here, HEAD_DIM) / denominator[..., None])
        .reshape(own_rows, local_width)
        .astype(jnp.bfloat16)
    )
    projected = jnp.dot(attention, out_weight, preferred_element_type=jnp.float32)
    feature_count = model_width // lax.axis_size("tp")
    summed_heads = lax.psum(projected, "tp")
    power = jnp.sum(summed_heads * summed_heads, axis=1)
    own_columns = lax.dynamic_slice_in_dim(summed_heads, tp_index * feature_count, feature_count, 1)
    normed = own_columns * lax.rsqrt(power / model_width + EPS)[:, None] * post_gain[None, :]
    residual_columns = lax.dynamic_slice_in_dim(
        hidden_in, tp_index * feature_count, feature_count, 1
    ).astype(jnp.float32)
    hidden_out = (residual_columns + normed).astype(jnp.bfloat16)
    leaf_onehot = (accepted_leaf[:, None] == jnp.arange(draft, dtype=jnp.int32)[None, :]).astype(
        jnp.float32
    )
    on_path = jnp.einsum("ri,rij->rj", leaf_onehot, ancestors, precision=lax.Precision.HIGHEST)
    target = cache_lengths[:, None] + tree_depth.astype(jnp.int32)
    placing = (places[None, :, None] == target[:, None, :]) & (on_path[:, None, :] > 0.5)
    written = jnp.any(placing, axis=-1)[..., None]
    placing_half = placing.astype(jnp.bfloat16)
    fresh_keys = jnp.einsum(
        "rpj,rjw->rpw",
        placing_half,
        keys.reshape(requests, draft, local_width),
        preferred_element_type=jnp.float32,
    ).astype(jnp.bfloat16)
    fresh_values = jnp.einsum(
        "rpj,rjw->rpw",
        placing_half,
        values.reshape(requests, draft, local_width),
        preferred_element_type=jnp.float32,
    ).astype(jnp.bfloat16)
    new_key_cache = jnp.where(written, fresh_keys, key_cache)
    new_value_cache = jnp.where(written, fresh_values, value_cache)
    return (hidden_out, new_key_cache, new_value_cache)


def solution(mesh):
    return jax.shard_map(
        body,
        mesh=mesh,
        in_specs=(
            P("seq", None),
            P(None, "tp"),
            P(None, "tp"),
            P(None, "tp"),
            P("tp", None),
            P("tp"),
            P("tp"),
            P("tp"),
            P(None, "seq", "tp"),
            P(None, "seq", "tp"),
            P(),
            P(),
            P(),
        ),
        out_specs=(P("seq", "tp"), P(None, "seq", "tp"), P(None, "seq", "tp")),
        check_vma=False,
    )
```

profile of v0, /device:TPU:2, one launch (start us, length us, event | category | flops | bytes accessed | tf_op | source)
XLA Modules:
  0.0 472.4 jit_solution(13318958439840656037)
XLA Ops:
  12.0 77.2 %all-gather.6.cloned.1.call-done = bf16[64,4,2048]{2,1,0:T(4,128)(2,1)} async-done(((bf16[1,4,2048]{2,1,0:T(4,128)(2,1)}), bf16[64,4,2048]{2,1,0:T(4,128)(2,1)}) %all-gather.6.cloned.1.call-update) | async-done | bytes 1048592 | tf_op jit(solution)/shard_map/all_gather | solution.py:102
  90.6 2.1 multiply_reduce_fusion
  92.7 2.1 multiply_reduce_fusion.1
  94.8 10.6 %all-reduce = (f32[256]{0:T(256)S(1)}, f32[256]{0:T(256)S(1)}) all-reduce(f32[256]{0:T(256)} %get-tuple-element.217, f32[256]{0:T(256)} %get-tuple-element.219), channel_id=1, replica_groups=mesh['seq'=64,'tp'=4] {'tp'}, use_global_device_ids=true, to_apply=%region_1.0 | all-reduce | flops 512 | bytes 4096 | tf_op jit(solution)/shard_map/psum | solution.py:114
  114.3 2.6 convolution_convert_fusion.2
  122.6 42.5 %all_gather.14 = f32[64,256,4]{1,2,0:T(4,128)S(1)} all-gather(f32[1,256,4]{1,2,0:T(4,128)S(1)} %all_gather_reshape.10), channel_id=1, replica_groups=mesh['seq'=64,'tp'=4] {'seq'}, dimensions={0}, use_global_device_ids=true | all-gather | bytes 266240 | tf_op jit(solution)/shard_map/all_gather | solution.py:14
  165.1 43.0 %all_gather.13 = f32[64,256,4]{1,2,0:T(4,128)S(1)} all-gather(f32[1,256,4]{1,2,0:T(4,128)S(1)} %all_gather_reshape.9), channel_id=1, replica_groups=mesh['seq'=64,'tp'=4] {'seq'}, dimensions={0}, use_global_device_ids=true | all-gather | bytes 266240 | tf_op jit(solution)/shard_map/all_gather | solution.py:14
  211.1 2.2 fusion.4
  213.3 2.0 fusion.3
  215.3 34.8 %all-gather.4.cloned.1.call-done = f32[64,256,512]{2,1,0:T(8,128)} async-done(((f32[1,256,512]{2,1,0:T(8,128)}), f32[64,256,512]{2,1,0:T(8,128)}) %all-gather.4.cloned.1.call-update) | async-done | bytes 33554448 | tf_op jit(solution)/shard_map/all_gather | solution.py:14
  251.1 193.7 %while.19 = (s32[]{:T(128)}, f32[256,4]{0,1:T(4,128)S(1)}, f32[256,4]{0,1:T(4,128)S(1)}, f32[256,512]{1,0:T(8,128)S(1)}, f32[64,256,4]{1,2,0:T(4,128)}, /*index=...) while((s32[]{:T(128)}, f32[256,4]{0,1:T(4,128)S(1)}, ...), condition=%wide.region_6.7_spmd, body=%wide.region_5.6_spmd.sunk | while | flops 399365 | bytes 3727503 | solution.py:20
  265.1 1.4 fusion.87
  280.5 1.4 fusion.87
  283.5 1.4 fusion.87
  286.6 1.4 fusion.87
  302.0 1.4 fusion.87
  305.0 1.4 fusion.87
  311.2 1.4 fusion.87
  320.4 1.4 fusion.87
  335.7 1.4 fusion.87
  341.9 1.4 fusion.87
  354.3 1.4 fusion.87
  445.2 2.0 fusion.59
  447.2 16.9 %psum.23 = f32[4,2048]{1,0:T(4,128)S(1)} all-reduce(f32[4,2048]{1,0:T(4,128)S(1)} %fusion.59), channel_id=1, replica_groups=mesh['seq'=64,'tp'=4] {'tp'}, use_global_device_ids=true, to_apply=%region_11.12 | all-reduce | flops 8192 | bytes 65536 | tf_op jit(solution)/shard_map/psum | solution.py:179
  (484 shorter events, 202.3 us)
Async XLA Ops:
  7.2 83.4 %copy-start = (bf16[2048,512]{1,0:T(8,128)(2,1)S(1)}, bf16[2048,512]{1,0:T(8,128)(2,1)}, u32[]{:S(2)}) copy-start(bf16[2048,512]{1,0:T(8,128)(2,1)} %param.17) | copy-start | bytes 6291460
  7.2 4.2 copy-start.23
  7.2 82.0 %all-gather.6.cloned.1.call-start = ((), (), s32[]{:S(2)}) async-start(), calls=%async_computation.1 | async-start | bytes 1064960 | tf_op jit(solution)/shard_map/all_gather | solution.py:102
  7.9 242.1 %all-gather.4.cloned.1.call-start = ((), (), s32[]{:S(2)}) async-start(), calls=%async_computation | async-start | bytes 34078720 | tf_op jit(solution)/shard_map/all_gather | solution.py:14
  11.4 81.3 %copy-start.15 = (s32[128]{0:T(128)}, s32[128]{0:T(128)S(1)}, u32[]{:S(2)}) copy-start(s32[128]{0:T(128)S(1)} %iota_add_fusion) | copy-start | bytes 1540
  11.5 97.4 %copy-start.21 = (pred[4,128]{1,0:T(4,128)(4,1)}, pred[4,128]{1,0:T(4,128)(4,1)S(1)}, u32[]{:S(2)}) copy-start(pred[4,128]{1,0:T(4,128)(4,1)S(1)} %broadcast_compare_fusion.1) | copy-start | bytes 1540
  90.6 4.2 copy-start.5
  92.7 13.2 %copy-start.19 = (f32[512]{0:T(512)S(1)}, f32[512]{0:T(512)}, u32[]{:S(2)}) copy-start(f32[512]{0:T(512)} %param.20) | copy-start | bytes 6148
  108.9 2.8 copy-start.26
  108.9 3.0 copy-start.24
  108.9 3.1 copy-start.16
  112.0 4.9 %copy-start.13 = (pred[4,64]{1,0:T(4,128)(4,1)}, pred[4,64]{1,0:T(4,128)(4,1)S(1)}, u32[]{:S(2)}) copy-start(pred[4,64]{1,0:T(4,128)(4,1)S(1)} %broadcast_compare_fusion) | copy-start | bytes 772
  113.7 4.0 copy-start.6
  113.7 4.0 copy-start.18
  113.7 4.0 copy-start.20
  118.3 3.2 copy-start.4
  118.4 92.6 %copy-start.2 = (bf16[4,128,512]{2,1,0:T(8,128)(2,1)S(1)}, bf16[4,128,512]{2,1,0:T(8,128)(2,1)}, u32[]{:S(2)}) copy-start(bf16[4,128,512]{2,1,0:T(8,128)(2,1)} %param.24) | copy-start | bytes 1572868
  118.5 92.6 %copy-start.14 = (pred[4,64]{1,0:T(4,128)(4,1)S(1)}, pred[4,64]{1,0:T(4,128)(4,1)}, u32[]{:S(2)}) copy-start(pred[4,64]{1,0:T(4,128)(4,1)} %copy-done.13) | copy-start | bytes 772
  122.5 90.8 %copy-start.8 = (bf16[4,128,512]{2,1,0:T(8,128)(2,1)S(1)}, bf16[4,128,512]{2,1,0:T(8,128)(2,1)}, u32[]{:S(2)}) copy-start(bf16[4,128,512]{2,1,0:T(8,128)(2,1)} %param.23) | copy-start | bytes 1572868
  165.1 46.0 %copy-start.10 = (f32[64,256,4]{1,2,0:T(4,128)}, f32[64,256,4]{1,2,0:T(4,128)S(1)}, u32[]{:S(2)}) copy-start(f32[64,256,4]{1,2,0:T(4,128)S(1)} %all_gather.14) | copy-start | bytes 786436
  208.1 2.9 copy-start.11
  251.1 193.8 %copy-start.12 = (bf16[64,4,128]{2,1,0:T(4,128)(2,1)S(1)}, bf16[64,4,128]{2,1,0:T(4,128)(2,1)}, u32[]{:S(2)}) copy-start(bf16[64,4,128]{2,1,0:T(4,128)(2,1)} %reshape.240) | copy-start | bytes 196612
  251.1 193.8 %copy-start.17 = (pred[4,64]{1,0:T(4,128)(4,1)S(1)}, pred[4,64]{1,0:T(4,128)(4,1)}, u32[]{:S(2)}) copy-start(pred[4,64]{1,0:T(4,128)(4,1)} %fusion.43) | copy-start | bytes 772
  444.8 19.3 %copy-start.22 = (f32[512]{0:T(512)S(1)}, f32[512]{0:T(512)}, u32[]{:S(2)}) copy-start(f32[512]{0:T(512)} %param.22) | copy-start | bytes 6148
  (5 other events, 6.0 us)
Sparse Core Ops, SparseCore 0:
  10.8 78.3 all-gather.5
  111.2 138.7 all-gather.3
where the time goes:
time: 478 us; the launch traced here: 472 us
  other arithmetic  141 us (29%)
  waiting for transfers between devices  113 us (24%)
  blocking collectives  113 us (24%)
  local copies, waits for them, and re-layouts  71 us (15%)
  matrix products  17.9 us (4%)
  between operations  14.6 us (3%)
    add x63, other arithmetic, join_partials(): out_first.reshape(rows_here, heads_here, -1) * scale_first[..., None]  87 us
    all_gather x2, blocking collectives, joined_2(): everything = jax.tree.map(lambda part: lax.all_gather(part, axis), x)  85.5 us
    all_gather x1, waiting for transfers between devices, body(): piece = lax.all_gather(hidden_in, 'seq', axis=0, tiled=True)  77.2 us
    add x64, other arithmetic, join_partials(): total_first * scale_first + total_second * scale_second  45 us
    all_gather x1, waiting for transfers between devices, joined_2(): everything = jax.tree.map(lambda part: lax.all_gather(part, axis), x)  34.8 us
    mul x63, local copies, waits for them, and re-layouts, join_partials(): out_first.reshape(rows_here, heads_here, -1) * scale_first[..., None]  21.1 us
    mul x63, local copies, waits for them, and re-layouts, join_partials(): out_second.reshape(rows_here, heads_here, -1) * scale_second[..., None]  21.1 us
    psum x1, blocking collectives, body(): summed_heads = lax.psum(projected, 'tp')  16.9 us
  transfers between devices with their start and end apart: 2, of which 2 were waited for; matrix products, arithmetic and copies ran while one was open for 5% of the time, Pallas kernels for 0%

commit v1 on v0

--- a/solution.py
+++ b/solution.py
@@ -99,7 +99,8 @@
     row_start = seq_index * own_rows
     ancestors, tree_depth = ancestry(parents)
     positions = (cache_lengths[:, None].astype(jnp.float32) + tree_depth).reshape(tokens)
-    piece = lax.all_gather(hidden_in, "seq", axis=0, tiled=True)
+    stack = jnp.stack([hidden_in] * lax.axis_size("seq"))
+    piece = jnp.concatenate(lax.all_to_all(stack, "seq", 0, 0), axis=0)
     raw = jnp.concatenate(
         [
             jnp.dot(piece, query_weight, preferred_element_type=jnp.float32),

time: 478 us -> 435 us (0.910)
  waiting for transfers between devices: 113 us -> 58.9 us
  starting transfers between devices: 0.08 us -> 12.1 us
    all_gather x1 -> x0, waiting for transfers between devices: 77.2 us -> none  [body(): piece = lax.all_gather(hidden_in, 'seq', axis=0, tiled=True)]
    all_to_all x0 -> x1, waiting for transfers between devices: none -> 24.5 us  [body(): piece = jnp.concatenate(lax.all_to_all(stack, 'seq', 0, 0), axis=0)]
    all_to_all x0 -> x1, starting transfers between devices: none -> 12 us  [body(): piece = jnp.concatenate(lax.all_to_all(stack, 'seq', 0, 0), axis=0)]
where the time goes in v1:
time: 435 us; the launch traced here: 430 us
  other arithmetic  139 us (32%)
  blocking collectives  113 us (26%)
  local copies, waits for them, and re-layouts  73.1 us (17%)
  waiting for transfers between devices  58.9 us (14%)
  matrix products  16.7 us (4%)
  between operations  14.6 us (3%)
  starting transfers between devices  12.1 us (3%)
    add x63, other arithmetic, join_partials(): out_first.reshape(rows_here, heads_here, -1) * scale_first[..., None]  87 us
    all_gather x2, blocking collectives, joined_2(): everything = jax.tree.map(lambda part: lax.all_gather(part, axis), x)  85.3 us
    add x64, other arithmetic, join_partials(): total_first * scale_first + total_second * scale_second  45 us
    all_gather x1, waiting for transfers between devices, joined_2(): everything = jax.tree.map(lambda part: lax.all_gather(part, axis), x)  34.4 us
    all_to_all x1, waiting for transfers between devices, body(): piece = jnp.concatenate(lax.all_to_all(stack, 'seq', 0, 0), axis=0)  24.5 us
    mul x63, local copies, waits for them, and re-layouts, join_partials(): out_first.reshape(rows_here, heads_here, -1) * scale_first[..., None]  21.1 us
    mul x63, local copies, waits for them, and re-layouts, join_partials(): out_second.reshape(rows_here, heads_here, -1) * scale_second[..., None]  21.1 us
    psum x1, blocking collectives, body(): summed_heads = lax.psum(projected, 'tp')  16.9 us
  transfers between devices with their start and end apart: 2, of which 2 were waited for; matrix products, arithmetic and copies ran while one was open for 5% of the time, Pallas kernels for 0%

profile of v1, /device:TPU:2, one launch (start us, length us, event | category | flops | bytes accessed | tf_op | source)
XLA Modules:
  0.0 429.6 jit_solution(12594305683040543119)
XLA Ops:
  7.2 2.4 stack.2
  9.6 12.0 %all-to-all-start = ((bf16[64,4,2048]{2,1,0:T(4,128)(2,1)}), bf16[64,4,2048]{2,1,0:T(4,128)(2,1)S(1)}, u32[]{:S(2)}, u32[]{:S(2)}) async-start(bf16[64,4,2048]{2,1,0:T(4,128)(2,1)} %stack.2), calls=%async_computation | async-start | bytes 2097152 | tf_op jit(solution)/shard_map/all_to_all | solution.py:103
  24.3 24.5 %all-to-all-done = bf16[64,4,2048]{2,1,0:T(4,128)(2,1)S(1)} async-done(((bf16[64,4,2048]{2,1,0:T(4,128)(2,1)}), bf16[64,4,2048]{2,1,0:T(4,128)(2,1)S(1)}, u32[]{:S(2)}, u32[]{:S(2)}) %all-to-all-start) | async-done | bytes 1048608 | tf_op jit(solution)/shard_map/all_to_all | solution.py:103
  49.8 2.9 multiply_reduce_fusion
  53.5 10.7 %all-reduce = (f32[256]{0:T(256)S(1)}, f32[256]{0:T(256)S(1)}) all-reduce(f32[256]{0:T(256)S(1)} %get-tuple-element.217, f32[256]{0:T(256)S(1)} %get-tuple-element.219), channel_id=1, replica_groups=mesh['seq'=64,'tp'=4] {'tp'}, use_global_device_ids=true, to_apply=%region_1.0 | all-reduce | flops 512 | bytes 4096 | tf_op jit(solution)/shard_map/psum | solution.py:115
  72.1 2.6 convolution_convert_fusion.2
  80.5 42.9 %all_gather.10 = f32[64,256,4]{1,2,0:T(4,128)S(1)} all-gather(f32[1,256,4]{1,2,0:T(4,128)S(1)} %all_gather_reshape.10), channel_id=1, replica_groups=mesh['seq'=64,'tp'=4] {'seq'}, dimensions={0}, use_global_device_ids=true | all-gather | bytes 266240 | tf_op jit(solution)/shard_map/all_gather | solution.py:14
  123.4 42.3 %all_gather.9 = f32[64,256,4]{1,2,0:T(4,128)S(1)} all-gather(f32[1,256,4]{1,2,0:T(4,128)S(1)} %all_gather_reshape.9), channel_id=1, replica_groups=mesh['seq'=64,'tp'=4] {'seq'}, dimensions={0}, use_global_device_ids=true | all-gather | bytes 266240 | tf_op jit(solution)/shard_map/all_gather | solution.py:14
  168.7 2.2 fusion.4
  171.0 2.0 fusion.3
  172.9 34.4 %all-gather.2.cloned.1.call-done = f32[64,256,512]{2,1,0:T(8,128)} async-done(((f32[1,256,512]{2,1,0:T(8,128)}), f32[64,256,512]{2,1,0:T(8,128)}) %all-gather.2.cloned.1.call-update) | async-done | bytes 33554448 | tf_op jit(solution)/shard_map/all_gather | solution.py:14
  208.4 193.7 %while.19 = (s32[]{:T(128)}, f32[256,4]{0,1:T(4,128)S(1)}, f32[256,4]{0,1:T(4,128)S(1)}, f32[256,512]{1,0:T(8,128)S(1)}, f32[64,256,4]{1,2,0:T(4,128)}, /*index=...) while((s32[]{:T(128)}, f32[256,4]{0,1:T(4,128)S(1)}, ...), condition=%wide.region_6.7_spmd, body=%wide.region_5.6_spmd.sunk | while | flops 399365 | bytes 3727503 | solution.py:20
  219.3 1.4 fusion.87
  231.6 1.4 fusion.87
  234.6 1.4 fusion.87
  250.0 1.4 fusion.87
  271.5 1.4 fusion.87
  274.6 1.4 fusion.87
  302.2 1.4 fusion.87
  308.4 1.4 fusion.87
  314.6 1.4 fusion.87
  320.8 1.4 fusion.87
  402.4 2.0 fusion.59
  404.4 16.9 %psum.23 = f32[4,2048]{1,0:T(4,128)S(1)} all-reduce(f32[4,2048]{1,0:T(4,128)S(1)} %fusion.59), channel_id=1, replica_groups=mesh['seq'=64,'tp'=4] {'tp'}, use_global_device_ids=true, to_apply=%region_11.12 | all-reduce | flops 8192 | bytes 65536 | tf_op jit(solution)/shard_map/psum | solution.py:180
  (486 shorter events, 201.0 us)
Async XLA Ops:
  7.2 42.7 %copy-start = (bf16[2048,512]{1,0:T(8,128)(2,1)S(1)}, bf16[2048,512]{1,0:T(8,128)(2,1)}, u32[]{:S(2)}) copy-start(bf16[2048,512]{1,0:T(8,128)(2,1)} %param.17) | copy-start | bytes 6291460
  7.2 14.5 %copy-start.24 = (s32[4]{0:T(128)S(1)}, s32[4]{0:T(128)}, u32[]{:S(2)}) copy-start(s32[4]{0:T(128)} %param.25) | copy-start | bytes 52
  7.2 14.5 %copy-start.23 = (s32[4,64]{1,0:T(4,128)S(1)}, s32[4,64]{1,0:T(4,128)}, u32[]{:S(2)}) copy-start(s32[4,64]{1,0:T(4,128)} %param.26) | copy-start | bytes 3076
  9.6 39.2 %all-to-all-start = ((bf16[64,4,2048]{2,1,0:T(4,128)(2,1)}), bf16[64,4,2048]{2,1,0:T(4,128)(2,1)S(1)}, u32[]{:S(2)}, u32[]{:S(2)}) async-start(bf16[64,4,2048]{2,1,0:T(4,128)(2,1)} %stack.2), calls=%async_computation | async-start | bytes 2097152 | tf_op jit(solution)/shard_map/all_to_all | solution.py:103
  21.6 185.7 %all-gather.2.cloned.1.call-start = ((), (), s32[]{:S(2)}) async-start(), calls=%async_computation.1 | async-start | bytes 34078720 | tf_op jit(solution)/shard_map/all_gather | solution.py:14
  23.6 29.1 %copy-start.15 = (s32[128]{0:T(128)}, s32[128]{0:T(128)S(1)}, u32[]{:S(2)}) copy-start(s32[128]{0:T(128)S(1)} %iota_add_fusion) | copy-start | bytes 1540
  23.7 43.0 %copy-start.21 = (pred[4,128]{1,0:T(4,128)(4,1)}, pred[4,128]{1,0:T(4,128)(4,1)S(1)}, u32[]{:S(2)}) copy-start(pred[4,128]{1,0:T(4,128)(4,1)S(1)} %broadcast_compare_fusion.1) | copy-start | bytes 1540
  49.8 2.9 copy-start.26
  52.7 12.1 %copy-start.19 = (f32[512]{0:T(512)S(1)}, f32[512]{0:T(512)}, u32[]{:S(2)}) copy-start(f32[512]{0:T(512)} %param.20) | copy-start | bytes 6148
  66.8 3.0 copy-start.25
  66.8 3.1 copy-start.16
  69.8 4.9 %copy-start.13 = (pred[4,64]{1,0:T(4,128)(4,1)}, pred[4,64]{1,0:T(4,128)(4,1)S(1)}, u32[]{:S(2)}) copy-start(pred[4,64]{1,0:T(4,128)(4,1)S(1)} %broadcast_compare_fusion) | copy-start | bytes 772
  71.5 4.0 copy-start.6
  71.5 4.0 copy-start.18
  71.5 4.0 copy-start.20
  76.1 3.1 copy-start.4
  76.3 92.4 %copy-start.2 = (bf16[4,128,512]{2,1,0:T(8,128)(2,1)S(1)}, bf16[4,128,512]{2,1,0:T(8,128)(2,1)}, u32[]{:S(2)}) copy-start(bf16[4,128,512]{2,1,0:T(8,128)(2,1)} %param.24) | copy-start | bytes 1572868
  76.3 92.4 %copy-start.14 = (pred[4,64]{1,0:T(4,128)(4,1)S(1)}, pred[4,64]{1,0:T(4,128)(4,1)}, u32[]{:S(2)}) copy-start(pred[4,64]{1,0:T(4,128)(4,1)} %copy-done.13) | copy-start | bytes 772
  80.4 90.6 %copy-start.8 = (bf16[4,128,512]{2,1,0:T(8,128)(2,1)S(1)}, bf16[4,128,512]{2,1,0:T(8,128)(2,1)}, u32[]{:S(2)}) copy-start(bf16[4,128,512]{2,1,0:T(8,128)(2,1)} %param.23) | copy-start | bytes 1572868
  123.4 45.3 %copy-start.10 = (f32[64,256,4]{1,2,0:T(4,128)}, f32[64,256,4]{1,2,0:T(4,128)S(1)}, u32[]{:S(2)}) copy-start(f32[64,256,4]{1,2,0:T(4,128)S(1)} %all_gather.10) | copy-start | bytes 786436
  165.7 2.9 copy-start.11
  208.4 193.8 %copy-start.12 = (bf16[64,4,128]{2,1,0:T(4,128)(2,1)S(1)}, bf16[64,4,128]{2,1,0:T(4,128)(2,1)}, u32[]{:S(2)}) copy-start(bf16[64,4,128]{2,1,0:T(4,128)(2,1)} %reshape.246) | copy-start | bytes 196612
  208.4 193.8 %copy-start.17 = (pred[4,64]{1,0:T(4,128)(4,1)S(1)}, pred[4,64]{1,0:T(4,128)(4,1)}, u32[]{:S(2)}) copy-start(pred[4,64]{1,0:T(4,128)(4,1)} %fusion.43) | copy-start | bytes 772
  402.1 19.3 %copy-start.22 = (f32[512]{0:T(512)S(1)}, f32[512]{0:T(512)}, u32[]{:S(2)}) copy-start(f32[512]{0:T(512)} %param.22) | copy-start | bytes 6148
  (6 other events, 9.5 us)
Sparse Core Ops, SparseCore 0:
  69.1 138.1 all-gather.1
